TPU v7x, 32 devices: a whole 2x2x4 slice. The times are simulated.
32 devices in a mesh: parts: 2 (over x), grid: 16 (over z, y, core).
Axes of the slice: x: 2, y: 2, z: 4, core: 2. Of those that a mesh axis runs over, the one named last changes fastest.
Arguments:
- field_modes: float32 [1771, 64, 256], P(None, ('parts', 'grid')), parts along dimension 1, may hold values from -6 to 6
- kl_coefficients: float32 [21, 64, 256], P(None, ('parts', 'grid')), parts along dimension 1, may hold values from 0.25 to 2
Outputs:
- applied_modes: float32 [1771, 64, 256], P(None, ('parts', 'grid')), parts along dimension 1
There are 2 independent parts, one for each index of `parts`. A program takes and returns all parts, laid end to end along the dimension named above; each array names one. Nothing has to cross between parts.
All inputs are finite; a program needn't handle non-finite values.
Results may differ from a plain program's by a relative error of at most 0.0001.
Values sent between devices are 32-bit elements; how exact they have to be, the bound alone decides.
A program may use at most 128 MiB of HBM per device.

v0:
```python
import math

import jax
import jax.numpy as jnp
import numpy as np
from jax import lax
from jax.sharding import PartitionSpec as P

VARS = 20
ORDER = 3


def padded_2(array, sides, width):
    for axis, dim in sides:
        size, length = (lax.axis_size(axis), array.shape[dim])
        up = [(i, (i + 1) % size) for i in range(size - 1)]
        down = [(j, i) for i, j in up]
        last = lax.slice_in_dim(array, length - width, length, axis=dim)
        first = lax.slice_in_dim(array, 0, width, axis=dim)
        before = lax.ppermute(last, axis, up)
        after = lax.ppermute(first, axis, down)
        array = jnp.concatenate([before, array, after], axis=dim)
    return array


def chaos_tables(nvars, order):
    levels = [[tuple([0] * nvars)]]
    for degree in range(1, order + 1):
        grown_set = set()
        for multi_index in levels[-1]:
            for variable in range(nvars):
                lifted = list(multi_index)
                lifted[variable] += 1
                grown_set.add(tuple(lifted))
        levels.append(sorted(grown_set, reverse=True))
    ordered = [multi_index for level_list in levels for multi_index in level_list]
    position = {multi_index: slot_index for slot_index, multi_index in enumerate(ordered)}
    modes_count = len(ordered)
    up_index = np.zeros((nvars, modes_count), np.int32)
    up_value = np.zeros((nvars, modes_count), np.float32)
    down_index = np.zeros((nvars, modes_count), np.int32)
    down_value = np.zeros((nvars, modes_count), np.float32)
    for slot_index, multi_index in enumerate(ordered):
        for variable in range(nvars):
            if sum(multi_index) < order:
                lifted = list(multi_index)
                lifted[variable] += 1
                up_index[variable, slot_index] = position[tuple(lifted)]
                up_value[variable, slot_index] = math.sqrt(multi_index[variable] + 1)
            if multi_index[variable] > 0:
                lowered = list(multi_index)
                lowered[variable] -= 1
                down_index[variable, slot_index] = position[tuple(lowered)]
                down_value[variable, slot_index] = math.sqrt(multi_index[variable])
    level_sizes = [len(level_list) for level_list in levels]
    return (up_index, up_value, down_index, down_value, level_sizes)


def five_point(extended, conduct):
    padded = jnp.pad(extended, [(0, 0)] * (extended.ndim - 1) + [(1, 1)])
    cpadded = jnp.pad(conduct, ((0, 0), (1, 1)))
    center = padded[..., 1:-1, 1:-1]
    center_coef = cpadded[1:-1, 1:-1]
    result = jnp.zeros(center.shape, jnp.float32)
    for row_cut, col_cut in (
        (slice(0, -2), slice(1, -1)),
        (slice(2, None), slice(1, -1)),
        (slice(1, -1), slice(0, -2)),
        (slice(1, -1), slice(2, None)),
    ):
        neighbour = padded[..., row_cut, col_cut]
        neighbour_coef = cpadded[row_cut, col_cut]
        result = result + 0.5 * (center_coef + neighbour_coef) * (center - neighbour)
    return result


def level_block(index_row, value_row, lower, upper, target_start, target_stop, flat):
    targets = jnp.arange(target_start, target_stop, dtype=jnp.int32)
    picked = index_row[lower:upper]
    weights = value_row[lower:upper]
    onehot = jnp.where(picked[:, None] == targets[None, :], weights[:, None], jnp.float32(0.0))
    return jnp.dot(
        onehot,
        flat[target_start:target_stop],
        preferred_element_type=jnp.float32,
        precision=lax.Precision.HIGHEST,
    )


def body(field_modes, kl_coefficients):
    modes_total = field_modes.shape[0]
    extended = padded_2(field_modes, (("grid", 1),), 1)
    coef_ext = padded_2(kl_coefficients, (("grid", 1),), 1)
    up_index, up_value, down_index, down_value, level_sizes = chaos_tables(VARS, ORDER)
    up_index = jnp.asarray(up_index, jnp.int32)
    down_index = jnp.asarray(down_index, jnp.int32)
    up_value = jnp.asarray(up_value, jnp.float32)
    down_value = jnp.asarray(down_value, jnp.float32)
    starts = [0]
    for count in level_sizes:
        starts.append(starts[-1] + count)
    running = five_point(extended, coef_ext[0])
    out_shape = running.shape
    running = running.reshape(modes_total, -1)

    def add_term(variable, running):
        conduct = lax.dynamic_index_in_dim(coef_ext, variable + 1, 0, keepdims=False)
        flat = five_point(extended, conduct).reshape(modes_total, -1)
        rows_up = lax.dynamic_index_in_dim(up_index, variable, 0, keepdims=False)
        rows_down = lax.dynamic_index_in_dim(down_index, variable, 0, keepdims=False)
        scale_up = lax.dynamic_index_in_dim(up_value, variable, 0, keepdims=False)
        scale_down = lax.dynamic_index_in_dim(down_value, variable, 0, keepdims=False)
        pieces = []
        for degree in range(len(level_sizes)):
            lower, upper = (starts[degree], starts[degree + 1])
            total = jnp.zeros((upper - lower, flat.shape[1]), jnp.float32)
            if degree + 1 < len(level_sizes):
                total = total + level_block(
                    rows_up, scale_up, lower, upper, starts[degree + 1], starts[degree + 2], flat
                )
            if degree > 0:
                total = total + level_block(
                    rows_down, scale_down, lower, upper, starts[degree - 1], starts[degree], flat
                )
            pieces.append(total)
        return running + jnp.concatenate(pieces, axis=0)

    running = lax.fori_loop(0, VARS, add_term, running)
    return running.reshape(out_shape)


def solution(mesh):
    placed = (P(None, ("parts", "grid"), None), P(None, ("parts", "grid"), None))
    return jax.shard_map(
        body,
        mesh=mesh,
        in_specs=placed,
        out_specs=P(None, ("parts", "grid"), None),
        check_vma=False,
    )
```

profile of v0, /device:TPU:9, one launch (start us, length us, event | category | flops | bytes accessed | tf_op | source)
XLA Modules:
  0.0 1163.6 jit_solution(8869528700239028973)
XLA Ops:
  0.0 7.3 fusion.75
  18.6 32.5 %collective-permute-done = f32[21,1,256]{2,1,0:T(1,128)S(1)} collective-permute-done((f32[21,1,256]{2,1,0:T(1,128)S(1)}, f32[21,1,256]{2,1,0:T(1,128)S(1)}, u32[]{:S(2)}, u32[]{:S(2)}) %collective-permute-start) | collective-permute-done | bytes 21536 | tf_op jit(solution)/shard_map/ppermute | solution.py:20
  52.8 6.5 pad_maximum_fusion
  59.4 18.4 %fusion.63 = (f32[1771,2,256]{2,1,0:T(2,128)}, f32[1771,2,256]{2,1,0:T(2,128)S(1)}, f32[1771,2,256]{2,1,0:T(2,128)}) fusion(f32[1771,2,256]{2,1,0:T(2,128)S(1)} %copy-done.2, f32[1771,1,256]{2,1,0:T(1,128)} %collective-permute-done.3, f32[2,256]{1,0:T(2,128)S(1)} %get-tuple-element.269, f32[1771,4,256]{2,1,0:T(4,128)S(1)} %pad_maximum_fusion, ...), kind=kLoop, calls=%fused_computation.85 | loop fusion | flops 11787776 | bytes 25397248 | tf_op jit(solution)/shard_map/sub | solution.py:73
  81.4 1076.9 %while.16 = (s32[]{:T(128)}, f32[1771,512]{1,0:T(8,128)}, f32[21,4,256]{2,1,0:T(4,128)S(1)}, f32[1771,2,256]{2,1,0:T(2,128)}, f32[1771,2,256]{2,1,0:T(2,128)}, /...) while((s32[]{:T(128)}, f32[1771,512]{1,0:T(8,128)}, ...), condition=%wide.region_1.2_spmd.clone, body=%wide.region_0.1_spmd.sunk.clone.sunk | while | flops 4036183552 | bytes 85362456 | solution.py:128
  90.5 16.1 %fusion.110 = f32[1771,2,256]{2,1,0:T(2,128)S(1)} fusion(f32[1771,4,256]{2,1,0:T(4,128)} %get-tuple-element.364, f32[1771,2,256]{2,1,0:T(2,128)} %get-tuple-element.363, f32[1771,2,256]{2,1,0:T(2,128)} %get-tuple-element.362, f32[2,256]{1,0:T(2,128)S(1)} %get-tuple-element.317, f32[2,256]{1,0:T(2,128)S(1)} %get-tuple-element.318, ...), kind=kLoop, calls=%fused_computation.5.clone.1 | loop fusion | flops 8160768 | bytes 21770240 | tf_op jit(solution)/shard_map/while/body/eval_jaxpr/add | solution.py:73
  118.2 11.1 concatenate.39
  144.3 16.1 %fusion.110 = f32[1771,2,256]{2,1,0:T(2,128)S(1)} fusion(f32[1771,4,256]{2,1,0:T(4,128)} %get-tuple-element.364, f32[1771,2,256]{2,1,0:T(2,128)} %get-tuple-element.363, f32[1771,2,256]{2,1,0:T(2,128)} %get-tuple-element.362, f32[2,256]{1,0:T(2,128)S(1)} %get-tuple-element.317, f32[2,256]{1,0:T(2,128)S(1)} %get-tuple-element.318, ...), kind=kLoop, calls=%fused_computation.5.clone.1 | loop fusion | flops 8160768 | bytes 21770240 | tf_op jit(solution)/shard_map/while/body/eval_jaxpr/add | solution.py:73
  172.1 11.1 concatenate.39
  183.2 5.9 add.366
  198.2 16.1 %fusion.110 = f32[1771,2,256]{2,1,0:T(2,128)S(1)} fusion(f32[1771,4,256]{2,1,0:T(4,128)} %get-tuple-element.364, f32[1771,2,256]{2,1,0:T(2,128)} %get-tuple-element.363, f32[1771,2,256]{2,1,0:T(2,128)} %get-tuple-element.362, f32[2,256]{1,0:T(2,128)S(1)} %get-tuple-element.317, f32[2,256]{1,0:T(2,128)S(1)} %get-tuple-element.318, ...), kind=kLoop, calls=%fused_computation.5.clone.1 | loop fusion | flops 8160768 | bytes 21770240 | tf_op jit(solution)/shard_map/while/body/eval_jaxpr/add | solution.py:73
  225.9 11.1 concatenate.39
  237.0 5.9 add.366
  252.0 16.1 %fusion.110 = f32[1771,2,256]{2,1,0:T(2,128)S(1)} fusion(f32[1771,4,256]{2,1,0:T(4,128)} %get-tuple-element.364, f32[1771,2,256]{2,1,0:T(2,128)} %get-tuple-element.363, f32[1771,2,256]{2,1,0:T(2,128)} %get-tuple-element.362, f32[2,256]{1,0:T(2,128)S(1)} %get-tuple-element.317, f32[2,256]{1,0:T(2,128)S(1)} %get-tuple-element.318, ...), kind=kLoop, calls=%fused_computation.5.clone.1 | loop fusion | flops 8160768 | bytes 21770240 | tf_op jit(solution)/shard_map/while/body/eval_jaxpr/add | solution.py:73
  279.8 11.1 concatenate.39
  290.8 5.9 add.366
  305.8 16.1 %fusion.110 = f32[1771,2,256]{2,1,0:T(2,128)S(1)} fusion(f32[1771,4,256]{2,1,0:T(4,128)} %get-tuple-element.364, f32[1771,2,256]{2,1,0:T(2,128)} %get-tuple-element.363, f32[1771,2,256]{2,1,0:T(2,128)} %get-tuple-element.362, f32[2,256]{1,0:T(2,128)S(1)} %get-tuple-element.317, f32[2,256]{1,0:T(2,128)S(1)} %get-tuple-element.318, ...), kind=kLoop, calls=%fused_computation.5.clone.1 | loop fusion | flops 8160768 | bytes 21770240 | tf_op jit(solution)/shard_map/while/body/eval_jaxpr/add | solution.py:73
  333.6 11.1 concatenate.39
  359.7 16.1 %fusion.110 = f32[1771,2,256]{2,1,0:T(2,128)S(1)} fusion(f32[1771,4,256]{2,1,0:T(4,128)} %get-tuple-element.364, f32[1771,2,256]{2,1,0:T(2,128)} %get-tuple-element.363, f32[1771,2,256]{2,1,0:T(2,128)} %get-tuple-element.362, f32[2,256]{1,0:T(2,128)S(1)} %get-tuple-element.317, f32[2,256]{1,0:T(2,128)S(1)} %get-tuple-element.318, ...), kind=kLoop, calls=%fused_computation.5.clone.1 | loop fusion | flops 8160768 | bytes 21770240 | tf_op jit(solution)/shard_map/while/body/eval_jaxpr/add | solution.py:73
  387.5 11.1 concatenate.39
  413.5 16.1 %fusion.110 = f32[1771,2,256]{2,1,0:T(2,128)S(1)} fusion(f32[1771,4,256]{2,1,0:T(4,128)} %get-tuple-element.364, f32[1771,2,256]{2,1,0:T(2,128)} %get-tuple-element.363, f32[1771,2,256]{2,1,0:T(2,128)} %get-tuple-element.362, f32[2,256]{1,0:T(2,128)S(1)} %get-tuple-element.317, f32[2,256]{1,0:T(2,128)S(1)} %get-tuple-element.318, ...), kind=kLoop, calls=%fused_computation.5.clone.1 | loop fusion | flops 8160768 | bytes 21770240 | tf_op jit(solution)/shard_map/while/body/eval_jaxpr/add | solution.py:73
  441.3 11.1 concatenate.39
  467.4 16.1 %fusion.110 = f32[1771,2,256]{2,1,0:T(2,128)S(1)} fusion(f32[1771,4,256]{2,1,0:T(4,128)} %get-tuple-element.364, f32[1771,2,256]{2,1,0:T(2,128)} %get-tuple-element.363, f32[1771,2,256]{2,1,0:T(2,128)} %get-tuple-element.362, f32[2,256]{1,0:T(2,128)S(1)} %get-tuple-element.317, f32[2,256]{1,0:T(2,128)S(1)} %get-tuple-element.318, ...), kind=kLoop, calls=%fused_computation.5.clone.1 | loop fusion | flops 8160768 | bytes 21770240 | tf_op jit(solution)/shard_map/while/body/eval_jaxpr/add | solution.py:73
  495.2 11.1 concatenate.39
  521.2 16.1 %fusion.110 = f32[1771,2,256]{2,1,0:T(2,128)S(1)} fusion(f32[1771,4,256]{2,1,0:T(4,128)} %get-tuple-element.364, f32[1771,2,256]{2,1,0:T(2,128)} %get-tuple-element.363, f32[1771,2,256]{2,1,0:T(2,128)} %get-tuple-element.362, f32[2,256]{1,0:T(2,128)S(1)} %get-tuple-element.317, f32[2,256]{1,0:T(2,128)S(1)} %get-tuple-element.318, ...), kind=kLoop, calls=%fused_computation.5.clone.1 | loop fusion | flops 8160768 | bytes 21770240 | tf_op jit(solution)/shard_map/while/body/eval_jaxpr/add | solution.py:73
  549.0 11.1 concatenate.39
  575.1 16.1 %fusion.110 = f32[1771,2,256]{2,1,0:T(2,128)S(1)} fusion(f32[1771,4,256]{2,1,0:T(4,128)} %get-tuple-element.364, f32[1771,2,256]{2,1,0:T(2,128)} %get-tuple-element.363, f32[1771,2,256]{2,1,0:T(2,128)} %get-tuple-element.362, f32[2,256]{1,0:T(2,128)S(1)} %get-tuple-element.317, f32[2,256]{1,0:T(2,128)S(1)} %get-tuple-element.318, ...), kind=kLoop, calls=%fused_computation.5.clone.1 | loop fusion | flops 8160768 | bytes 21770240 | tf_op jit(solution)/shard_map/while/body/eval_jaxpr/add | solution.py:73
  602.8 11.1 concatenate.39
  628.9 16.1 %fusion.110 = f32[1771,2,256]{2,1,0:T(2,128)S(1)} fusion(f32[1771,4,256]{2,1,0:T(4,128)} %get-tuple-element.364, f32[1771,2,256]{2,1,0:T(2,128)} %get-tuple-element.363, f32[1771,2,256]{2,1,0:T(2,128)} %get-tuple-element.362, f32[2,256]{1,0:T(2,128)S(1)} %get-tuple-element.317, f32[2,256]{1,0:T(2,128)S(1)} %get-tuple-element.318, ...), kind=kLoop, calls=%fused_computation.5.clone.1 | loop fusion | flops 8160768 | bytes 21770240 | tf_op jit(solution)/shard_map/while/body/eval_jaxpr/add | solution.py:73
  656.7 11.1 concatenate.39
  682.8 16.1 %fusion.110 = f32[1771,2,256]{2,1,0:T(2,128)S(1)} fusion(f32[1771,4,256]{2,1,0:T(4,128)} %get-tuple-element.364, f32[1771,2,256]{2,1,0:T(2,128)} %get-tuple-element.363, f32[1771,2,256]{2,1,0:T(2,128)} %get-tuple-element.362, f32[2,256]{1,0:T(2,128)S(1)} %get-tuple-element.317, f32[2,256]{1,0:T(2,128)S(1)} %get-tuple-element.318, ...), kind=kLoop, calls=%fused_computation.5.clone.1 | loop fusion | flops 8160768 | bytes 21770240 | tf_op jit(solution)/shard_map/while/body/eval_jaxpr/add | solution.py:73
  710.5 11.1 concatenate.39
  736.6 16.1 %fusion.110 = f32[1771,2,256]{2,1,0:T(2,128)S(1)} fusion(f32[1771,4,256]{2,1,0:T(4,128)} %get-tuple-element.364, f32[1771,2,256]{2,1,0:T(2,128)} %get-tuple-element.363, f32[1771,2,256]{2,1,0:T(2,128)} %get-tuple-element.362, f32[2,256]{1,0:T(2,128)S(1)} %get-tuple-element.317, f32[2,256]{1,0:T(2,128)S(1)} %get-tuple-element.318, ...), kind=kLoop, calls=%fused_computation.5.clone.1 | loop fusion | flops 8160768 | bytes 21770240 | tf_op jit(solution)/shard_map/while/body/eval_jaxpr/add | solution.py:73
  764.4 11.1 concatenate.39
  790.4 16.1 %fusion.110 = f32[1771,2,256]{2,1,0:T(2,128)S(1)} fusion(f32[1771,4,256]{2,1,0:T(4,128)} %get-tuple-element.364, f32[1771,2,256]{2,1,0:T(2,128)} %get-tuple-element.363, f32[1771,2,256]{2,1,0:T(2,128)} %get-tuple-element.362, f32[2,256]{1,0:T(2,128)S(1)} %get-tuple-element.317, f32[2,256]{1,0:T(2,128)S(1)} %get-tuple-element.318, ...), kind=kLoop, calls=%fused_computation.5.clone.1 | loop fusion | flops 8160768 | bytes 21770240 | tf_op jit(solution)/shard_map/while/body/eval_jaxpr/add | solution.py:73
  818.2 11.1 concatenate.39
  844.3 16.1 %fusion.110 = f32[1771,2,256]{2,1,0:T(2,128)S(1)} fusion(f32[1771,4,256]{2,1,0:T(4,128)} %get-tuple-element.364, f32[1771,2,256]{2,1,0:T(2,128)} %get-tuple-element.363, f32[1771,2,256]{2,1,0:T(2,128)} %get-tuple-element.362, f32[2,256]{1,0:T(2,128)S(1)} %get-tuple-element.317, f32[2,256]{1,0:T(2,128)S(1)} %get-tuple-element.318, ...), kind=kLoop, calls=%fused_computation.5.clone.1 | loop fusion | flops 8160768 | bytes 21770240 | tf_op jit(solution)/shard_map/while/body/eval_jaxpr/add | solution.py:73
  872.1 11.1 concatenate.39
  898.1 16.1 %fusion.110 = f32[1771,2,256]{2,1,0:T(2,128)S(1)} fusion(f32[1771,4,256]{2,1,0:T(4,128)} %get-tuple-element.364, f32[1771,2,256]{2,1,0:T(2,128)} %get-tuple-element.363, f32[1771,2,256]{2,1,0:T(2,128)} %get-tuple-element.362, f32[2,256]{1,0:T(2,128)S(1)} %get-tuple-element.317, f32[2,256]{1,0:T(2,128)S(1)} %get-tuple-element.318, ...), kind=kLoop, calls=%fused_computation.5.clone.1 | loop fusion | flops 8160768 | bytes 21770240 | tf_op jit(solution)/shard_map/while/body/eval_jaxpr/add | solution.py:73
  925.9 11.1 concatenate.39
  952.0 16.1 %fusion.110 = f32[1771,2,256]{2,1,0:T(2,128)S(1)} fusion(f32[1771,4,256]{2,1,0:T(4,128)} %get-tuple-element.364, f32[1771,2,256]{2,1,0:T(2,128)} %get-tuple-element.363, f32[1771,2,256]{2,1,0:T(2,128)} %get-tuple-element.362, f32[2,256]{1,0:T(2,128)S(1)} %get-tuple-element.317, f32[2,256]{1,0:T(2,128)S(1)} %get-tuple-element.318, ...), kind=kLoop, calls=%fused_computation.5.clone.1 | loop fusion | flops 8160768 | bytes 21770240 | tf_op jit(solution)/shard_map/while/body/eval_jaxpr/add | solution.py:73
  979.8 11.1 concatenate.39
  1005.8 16.1 %fusion.110 = f32[1771,2,256]{2,1,0:T(2,128)S(1)} fusion(f32[1771,4,256]{2,1,0:T(4,128)} %get-tuple-element.364, f32[1771,2,256]{2,1,0:T(2,128)} %get-tuple-element.363, f32[1771,2,256]{2,1,0:T(2,128)} %get-tuple-element.362, f32[2,256]{1,0:T(2,128)S(1)} %get-tuple-element.317, f32[2,256]{1,0:T(2,128)S(1)} %get-tuple-element.318, ...), kind=kLoop, calls=%fused_computation.5.clone.1 | loop fusion | flops 8160768 | bytes 21770240 | tf_op jit(solution)/shard_map/while/body/eval_jaxpr/add | solution.py:73
  1033.6 11.1 concatenate.39
  1059.7 16.1 %fusion.110 = f32[1771,2,256]{2,1,0:T(2,128)S(1)} fusion(f32[1771,4,256]{2,1,0:T(4,128)} %get-tuple-element.364, f32[1771,2,256]{2,1,0:T(2,128)} %get-tuple-element.363, f32[1771,2,256]{2,1,0:T(2,128)} %get-tuple-element.362, f32[2,256]{1,0:T(2,128)S(1)} %get-tuple-element.317, f32[2,256]{1,0:T(2,128)S(1)} %get-tuple-element.318, ...), kind=kLoop, calls=%fused_computation.5.clone.1 | loop fusion | flops 8160768 | bytes 21770240 | tf_op jit(solution)/shard_map/while/body/eval_jaxpr/add | solution.py:73
  1087.4 11.1 concatenate.39
  1113.5 16.1 %fusion.110 = f32[1771,2,256]{2,1,0:T(2,128)S(1)} fusion(f32[1771,4,256]{2,1,0:T(4,128)} %get-tuple-element.364, f32[1771,2,256]{2,1,0:T(2,128)} %get-tuple-element.363, f32[1771,2,256]{2,1,0:T(2,128)} %get-tuple-element.362, f32[2,256]{1,0:T(2,128)S(1)} %get-tuple-element.317, f32[2,256]{1,0:T(2,128)S(1)} %get-tuple-element.318, ...), kind=kLoop, calls=%fused_computation.5.clone.1 | loop fusion | flops 8160768 | bytes 21770240 | tf_op jit(solution)/shard_map/while/body/eval_jaxpr/add | solution.py:73
  1141.3 11.1 concatenate.39
  (717 shorter events, 534.0 us)
Async XLA Ops:
  0.0 13.0 %copy-start.3 = (f32[21,2,256]{2,1,0:T(2,128)S(1)}, f32[21,2,256]{2,1,0:T(2,128)}, u32[]{:S(2)}) copy-start(f32[21,2,256]{2,1,0:T(2,128)} %param.9) | copy-start | bytes 129028
  7.3 45.4 %collective-permute-start.1 = (f32[1771,1,256]{2,1,0:T(1,128)}, f32[1771,1,256]{2,1,0:T(1,128)S(1)}, u32[]{:S(2)}, u32[]{:S(2)}) collective-permute-start(f32[1771,1,256]{2,1,0:T(1,128)} %get-tuple-element.266), channel_id=1, source_target_pairs={{0,1},{1,2},{2,3},{3,4},{4,5},{5,6},{6,7},{7,8},{8,9},{9,10},{10,1... | collective-permute-start | bytes 5440520 | tf_op jit(solution)/shard_map/ppermute | solution.py:20
  11.0 41.7 %collective-permute-start.3 = (f32[1771,1,256]{2,1,0:T(1,128)}, f32[1771,1,256]{2,1,0:T(1,128)}, u32[]{:S(2)}, u32[]{:S(2)}) collective-permute-start(f32[1771,1,256]{2,1,0:T(1,128)} %get-tuple-element.267), channel_id=1, source_target_pairs={{1,0},{2,1},{3,2},{4,3},{5,4},{6,5},{7,6},{8,7},{9,8},{10,9},{11,1... | collective-permute-start | bytes 5440520 | tf_op jit(solution)/shard_map/ppermute | solution.py:21
  13.0 38.0 %collective-permute-start = (f32[21,1,256]{2,1,0:T(1,128)S(1)}, f32[21,1,256]{2,1,0:T(1,128)S(1)}, u32[]{:S(2)}, u32[]{:S(2)}) collective-permute-start(f32[21,1,256]{2,1,0:T(1,128)S(1)} %get-tuple-element.272), channel_id=1, source_target_pairs={{0,1},{1,2},{2,3},{3,4},{4,5},{5,6},{6,7},{7,8},{8,9},{9,10},{10,1... | collective-permute-start | bytes 64520 | tf_op jit(solution)/shard_map/ppermute | solution.py:20
  16.7 36.0 %collective-permute-start.2 = (f32[21,1,256]{2,1,0:T(1,128)S(1)}, f32[21,1,256]{2,1,0:T(1,128)S(1)}, u32[]{:S(2)}, u32[]{:S(2)}) collective-permute-start(f32[21,1,256]{2,1,0:T(1,128)S(1)} %get-tuple-element.273), channel_id=1, source_target_pairs={{1,0},{2,1},{3,2},{4,3},{5,4},{6,5},{7,6},{8,7},{9,8},{10,9},{11,1... | collective-permute-start | bytes 64520 | tf_op jit(solution)/shard_map/ppermute | solution.py:21
  52.8 6.6 copy-start.2
  59.3 18.5 %copy-start = (f32[1771,4,256]{2,1,0:T(4,128)}, f32[1771,4,256]{2,1,0:T(4,128)S(1)}, u32[]{:S(2)}) copy-start(f32[1771,4,256]{2,1,0:T(4,128)S(1)} %pad_maximum_fusion) | copy-start | bytes 21762052
  106.6 3.2 copy-start.1
  111.0 4.0 slice-start
  160.5 3.2 copy-start.1
  164.8 4.0 slice-start
  214.3 3.2 copy-start.1
  218.7 4.0 slice-start
  268.1 3.2 copy-start.1
  272.5 4.0 slice-start
  322.0 3.2 copy-start.1
  326.4 4.0 slice-start
  375.8 3.2 copy-start.1
  380.2 4.0 slice-start
  429.7 3.2 copy-start.1
  434.1 4.0 slice-start
  483.5 3.2 copy-start.1
  487.9 4.0 slice-start
  537.4 3.2 copy-start.1
  541.7 4.0 slice-start
  591.2 3.2 copy-start.1
  595.6 4.0 slice-start
  645.0 3.2 copy-start.1
  649.4 4.0 slice-start
  698.9 3.2 copy-start.1
  703.3 4.0 slice-start
  752.7 3.2 copy-start.1
  757.1 4.0 slice-start
  806.6 3.2 copy-start.1
  811.0 4.0 slice-start
  860.4 3.2 copy-start.1
  864.8 4.0 slice-start
  914.3 3.2 copy-start.1
  918.7 4.0 slice-start
  968.1 3.2 copy-start.1
  972.5 4.0 slice-start
  1022.0 3.2 copy-start.1
  1026.3 4.0 slice-start
  1075.8 3.2 copy-start.1
  1080.2 4.0 slice-start
  1129.6 3.2 copy-start.1
  1134.0 4.0 slice-start
where the time goes:
time: 1190 us; the launch traced here: 1160 us
  other arithmetic  483 us (41%)
  local copies, waits for them, and re-layouts  458 us (38%)
  matrix products  173 us (15%)
  waiting for transfers between devices  34 us (3%)
    add x20, other arithmetic, five_point(): result + 0.5 * (center_coef + neighbour_coef) * (center - neighbour)  323 us
    concatenate x20, local copies, waits for them, and re-layouts, add_term(): return running + jnp.concatenate(pieces, axis=0)  221 us
    dot_general x100, matrix products, level_block(): jnp.dot(onehot, flat[target_start:target_stop], preferred_element_type=jn...  173 us
    add x20, other arithmetic, add_term(): return running + jnp.concatenate(pieces, axis=0)  118 us
    slice x80, local copies, waits for them, and re-layouts, level_block(): picked = index_row[lower:upper]  74.5 us
    slice x80, local copies, waits for them, and re-layouts, level_block(): weights = value_row[lower:upper]  74.1 us
    while x200, local copies, waits for them, and re-layouts  33.8 us
    ppermute x2, waiting for transfers between devices, padded_2(): before = lax.ppermute(last, axis, up)  32.5 us
  transfers between devices with their start and end apart: 4, of which 2 were waited for; matrix products, arithmetic and copies ran while one was open for 0% of the time, Pallas kernels for 0%

commit v1 on v0

v1 whole, which is shorter than its diff:
```python
import math

import jax
import jax.numpy as jnp
from jax import lax
from jax.experimental import pallas as pl
from jax.experimental.pallas import tpu as pltpu
from jax.sharding import PartitionSpec as P

VARS = 20
R2 = math.sqrt(2.0)
R6 = math.sqrt(6.0)
LANES = 128


def tri(n):
    return n * (n + 1) // 2


def idx2(i, j):
    return 1 + VARS + tri(VARS) - tri(VARS - i) + j - i


def idx3(i, j, k):
    first = 1 + VARS + tri(VARS)
    total = VARS * (VARS + 1) * (VARS + 2) // 6
    rest = VARS - i
    off = total - rest * (rest + 1) * (rest + 2) // 6
    return first + off + tri(VARS - i) - tri(VARS - j) + k - j


DEG2 = 1 + VARS
NPAIR = tri(VARS)
DEG3 = DEG2 + NPAIR
GROUP = 4


def start_low(load, w, u2, acc_a, acc_b, store):
    w0 = w(0)
    u0 = load(0)
    zero = jnp.zeros_like(u0)
    out0 = w0 * u0
    for v in range(VARS):
        out0 = out0 + w(1 + v) * load(1 + v)
    for i in range(VARS):
        for j in range(i, VARS):
            val = load(idx2(i, j))
            if i == j:
                val = val * R2
            u2[idx2(i, j) - DEG2] = val
    ones = []
    for i in range(VARS):
        total = w0 * load(1 + i) + w(1 + i) * u0
        for v in range(VARS):
            total = total + w(1 + v) * u2[idx2(min(i, v), max(i, v)) - DEG2]
        ones.append(total)
        for j in range(i, VARS):
            pos = idx2(i, j) - DEG2
            acc_a[pos] = w0 * u2[pos] + w(1 + i) * load(1 + j) + w(1 + j) * load(1 + i)
            acc_b[pos] = zero
        if i % 5 == 4:
            for n, t in enumerate(ones):
                u2[NPAIR + i - 4 + n] = t
            ones = []
    return out0


def pair_row(load, w, u2, acc_a, acc_b, store, i, j, base, b2i, same):
    w0 = w(0)
    wi = w(1 + i)
    wj = w(1 + j)
    uij = u2[b2i + j]
    total = None
    for lo in range(j, VARS, GROUP):
        ks = range(lo, min(lo + GROUP, VARS))
        u3, outs, ia, jb = [], [], [], []
        for k in ks:
            scale = (R6 if same else R2) if k == j else (R2 if same else None)
            val = load(base + (k - j))
            if scale is not None:
                val = val * scale
            wk = w(1 + k)
            out = w0 * val + wi * u2[idx2(j, k) - DEG2] + wj * u2[b2i + k] + wk * uij
            if scale is not None:
                out = out * (1.0 / scale)
            outs.append(out)
            term = wk * val
            total = term if total is None else total + term
            if k != j:
                ia.append(acc_a[b2i + k] + wj * val)
            if not same:
                jb.append(acc_b[idx2(j, k) - DEG2] + wi * val)
        for n, k in enumerate(ks):
            store(base + (k - j), outs[n])
            if k != j:
                acc_a[b2i + k] = ia.pop(0)
            if not same:
                acc_b[idx2(j, k) - DEG2] = jb.pop(0)
    acc_a[b2i + j] = acc_a[b2i + j] + total


def cubic(load, w, u2, acc_a, acc_b, store, i_lo, i_hi):
    for j in range(i_lo, VARS):
        hi = min(j, i_hi)

        def step(i, carry):
            base, b2i = carry
            pair_row(load, w, u2, acc_a, acc_b, store, i, j, base, b2i, False)
            left = VARS - 1 - i
            return base + jnp.right_shift(left * (left + 1), 1), b2i + left

        if hi > i_lo:
            lax.fori_loop(
                i_lo,
                hi,
                step,
                (jnp.int32(idx3(i_lo, j, j)), jnp.int32(idx2(i_lo, i_lo) - DEG2 - i_lo)),
            )
        if j < i_hi:
            pair_row(
                load, w, u2, acc_a, acc_b, store, j, j, idx3(j, j, j), idx2(j, j) - DEG2 - j, True
            )


def finish_low(out0, u2, acc_a, acc_b, store):
    store(0, out0)
    for i in range(VARS):
        store(1 + i, u2[NPAIR + i])
        for j in range(i, VARS):
            pos = idx2(i, j) - DEG2
            out = acc_a[pos] + acc_b[pos]
            if i == j:
                out = out * (1.0 / R2)
            store(DEG2 + pos, out)


def shifted(g):
    lane = lax.broadcasted_iota(jnp.int32, g.shape, 1)
    row = lax.broadcasted_iota(jnp.int32, g.shape, 0)
    second = (row & 2) == 2
    left = pltpu.roll(g, LANES - 1, 1)
    east = jnp.where(lane < LANES - 1, left, jnp.where(second, 0.0, pltpu.roll(left, 6, 0)))
    right = pltpu.roll(g, 1, 1)
    west = jnp.where(lane > 0, right, jnp.where(second, pltpu.roll(right, 2, 0), 0.0))
    other = jnp.where((row & 1) == 0, pltpu.roll(g, 7, 0), pltpu.roll(g, 1, 0))
    return east, west, other


def spread(first, second):
    row = lax.broadcasted_iota(jnp.int32, first.shape, 0)
    return (
        jnp.where(row < 4, first, pltpu.roll(second, 4, 0)),
        jnp.where(row < 4, pltpu.roll(first, 4, 0), second),
    )


def local_kernel(modes, f_ref, c_ref, h_ref, o_ref, u_ref, w_ref, u2, acc_a, acc_b):
    terms = 1 + VARS

    def weights(n, _):
        at = jnp.minimum(2 * n, terms - 2)
        c = c_ref[pl.ds(at, 2)].reshape(8, LANES)
        h = h_ref[pl.ds(at, 2)].reshape(8, LANES)
        east, west, other = shifted(c)
        center = 0.5 * (4.0 * c + east + west + other + h)
        a0, a1 = spread(center, -0.5 * (c + east))
        b0, b1 = spread(-0.5 * (c + west), -0.5 * (c + other))
        w_ref[0, at] = a0
        w_ref[0, at + 1] = a1
        w_ref[1, at] = b0
        w_ref[1, at + 1] = b1
        return 0

    lax.fori_loop(0, (terms + 1) // 2, weights, 0)

    def build(n, _):
        at = jnp.minimum(2 * n, modes - 2)
        g = f_ref[pl.ds(at, 2)].reshape(8, LANES)
        east, west, other = shifted(g)
        a0, a1 = spread(g, east)
        b0, b1 = spread(west, other)
        u_ref[0, at] = a0
        u_ref[0, at + 1] = a1
        u_ref[1, at] = b0
        u_ref[1, at + 1] = b1
        return 0

    lax.fori_loop(0, (modes + 1) // 2, build, 0)

    def half(n, _):
        load = lambda m: u_ref[n, m]
        w = lambda t: w_ref[n, t]

        def store(m, value):
            u_ref[n, m] = value

        out0 = start_low(load, w, u2, acc_a, acc_b, store)
        cubic(load, w, u2, acc_a, acc_b, store, 0, VARS)
        finish_low(out0, u2, acc_a, acc_b, store)
        return 0

    lax.fori_loop(0, 2, half, 0)

    def total(m, _):
        both = u_ref[0, m] + u_ref[1, m]
        o_ref[m] = both[0:4] + both[4:8]
        return 0

    lax.fori_loop(0, modes, total, 0, unroll=7)


def halo_kernel(modes, a_ref, g_ref, c_ref, h_ref, o_ref, w_ref, u2, acc_a, acc_b):
    w_ref[...] = -0.5 * (c_ref[...] + h_ref[...])
    load = lambda m: g_ref[m]
    w = lambda t: w_ref[t]

    def store(m, value):
        o_ref[m] = a_ref[m] + value

    out0 = start_low(load, w, u2, acc_a, acc_b, store)
    cubic(load, w, u2, acc_a, acc_b, store, 0, VARS)
    finish_low(out0, u2, acc_a, acc_b, store)


def tiled(array):
    n = array.shape[0]
    return array.reshape(n, 2, 2, LANES).transpose(0, 2, 1, 3).reshape(n, 4, LANES)


def exchange(array):
    size = lax.axis_size("grid")
    up = [(i, i + 1) for i in range(size - 1)]
    down = [(i + 1, i) for i in range(size - 1)]
    n = array.shape[0]
    four = array.reshape(n, 2, 2, LANES)
    above = lax.ppermute(four[:, 1], "grid", up)
    below = lax.ppermute(four[:, 0], "grid", down)
    return above, below


def merge(above, below):
    return jnp.stack([above, below], axis=2).reshape(above.shape[0], 4, LANES)


def body(field, coef):
    modes = field.shape[0]
    c4 = tiled(coef)
    f4 = tiled(field)
    hc = merge(*exchange(coef))
    above, below = exchange(field)
    params = pltpu.CompilerParams(vmem_limit_bytes=48 * 1024 * 1024)
    low = lambda s: [pltpu.VMEM((NPAIR + VARS, s, LANES), jnp.float32)] + [
        pltpu.VMEM((NPAIR, s, LANES), jnp.float32)
    ] * 2
    part = pl.pallas_call(
        lambda *refs: local_kernel(modes, *refs),
        out_shape=jax.ShapeDtypeStruct((modes, 4, LANES), jnp.float32),
        scratch_shapes=[
            pltpu.VMEM((2, modes, 8, LANES), jnp.float32),
            pltpu.VMEM((2, 1 + VARS, 8, LANES), jnp.float32),
        ]
        + low(8),
        compiler_params=params,
        cost_estimate=pl.CostEstimate(
            flops=40 * 10**6, bytes_accessed=40 * 10**6, transcendentals=0
        ),
        name="local",
    )(f4, c4, hc)
    out = pl.pallas_call(
        lambda *refs: halo_kernel(modes, *refs),
        out_shape=jax.ShapeDtypeStruct((modes, 4, LANES), jnp.float32),
        scratch_shapes=[pltpu.VMEM((1 + VARS, 4, LANES), jnp.float32)] + low(4),
        compiler_params=params,
        name="halo",
    )(part, merge(above, below), c4, hc)
    return out.reshape(modes, 2, 2, LANES).transpose(0, 2, 1, 3).reshape(field.shape)


def solution(mesh):
    placed = P(None, ("parts", "grid"), None)
    return jax.shard_map(
        body, mesh=mesh, in_specs=(placed, placed), out_specs=placed, check_vma=False
    )
```

time: 1190 us -> 151 us (0.13); the launches traced: 1160 us -> 151 us
  other arithmetic: 483 us -> 6.22 us
  local copies, waits for them, and re-layouts: 458 us -> 9.76 us
  matrix products: 173 us -> 0 us
  Pallas kernels: 0 us -> 89.6 us
    add x100 -> x0, other arithmetic: 441 us -> none  [the longest x20 323 us: five_point(): result + 0.5 * (center_coef + neighbour_coef) * (center - neighbour)]
    concatenate x20 -> x0, local copies, waits for them, and re-layouts: 221 us -> none  [add_term(): return running + jnp.concatenate(pieces, axis=0)]
    slice x242 -> x0, local copies, waits for them, and re-layouts: 179 us -> none  [the longest x80 74.5 us: level_block(): picked = index_row[lower:upper]]
    dot_general x100 -> x0, matrix products: 173 us -> none  [level_block(): jnp.dot(onehot, flat[target_start:target_stop], preferred_element_type=jn...]
    pallas_call x0 -> x2, Pallas kernels: none -> 89.6 us  [the longest x1 80.8 us: body(): pl.pallas_call(lambda *refs: local_kernel(modes, *refs), out_shape=jax.Sh...]
    while x200 -> x0, local copies, waits for them, and re-layouts: 33.8 us -> none
    sub x1 -> x0, other arithmetic: 18.4 us -> none  [five_point(): center - neighbour]
    select_n x20 -> x0, other arithmetic: 15.9 us -> none  [level_block(): jnp.where(picked[:, None] == targets[None, :], weights[:, None], jnp.floa...]
  transfers between devices with their start and end apart: 4 -> 4, of which waited for: 2 -> 2; matrix products, arithmetic and copies ran while one was open for 0% -> 0% of each run, Pallas kernels for 0% -> 54%
where the time goes in v1:
time: 151 us
  Pallas kernels  89.6 us (59%)
  waiting for transfers between devices  34 us (23%)
  starting transfers between devices  11.2 us (7%)
  local copies, waits for them, and re-layouts  9.76 us (6%)
  other arithmetic  6.22 us (4%)
    pallas_call x1, Pallas kernels, body(): pl.pallas_call(lambda *refs: local_kernel(modes, *refs), out_shape=jax.Sh...  80.8 us
    ppermute x2, waiting for transfers between devices, exchange(): above = lax.ppermute(four[:, 1], 'grid', up)  32.4 us
    pallas_call x1, Pallas kernels, body(): pl.pallas_call(lambda *refs: halo_kernel(modes, *refs), out_shape=jax.Sha...  8.76 us
    ppermute x2, starting transfers between devices, exchange(): above = lax.ppermute(four[:, 1], 'grid', up)  7.34 us
    reshape x2, local copies, waits for them, and re-layouts, tiled(): array.reshape(n, 2, 2, LANES).transpose(0, 2, 1, 3).reshape(n, 4, LANES)  6.68 us
    another operation x2, other arithmetic, merge(): return jnp.stack([above, below], axis=2).reshape(above.shape[0], 4, LANES)  6.22 us
    ppermute x2, starting transfers between devices, exchange(): below = lax.ppermute(four[:, 0], 'grid', down)  3.84 us
    squeeze x2, local copies, waits for them, and re-layouts, exchange(): above = lax.ppermute(four[:, 1], 'grid', up)  3.08 us
  transfers between devices with their start and end apart: 4, of which 2 were waited for; matrix products, arithmetic and copies ran while one was open for 0% of the time, Pallas kernels for 54%

profile of v1, /device:TPU:9, one launch (start us, length us, event | category | flops | bytes accessed | tf_op | source)
XLA Modules:
  0.0 150.8 jit_solution(17244172446306389824)
XLA Ops:
  0.0 6.6 %reshape.26 = f32[1771,2,2,128]{3,2,1,0:T(2,128)} reshape(f32[1771,2,256]{2,1,0:T(2,128)} %param.2) | data formatting | bytes 7254016 | tf_op jit(solution)/shard_map/reshape | solution.py:227
  6.6 0.0 copy-start
  6.6 3.1 %slice_bitcast_fusion.1 = (f32[1771,2,128]{2,1,0:T(2,128)}, f32[1771,2,128]{2,1,0:T(2,128)S(1)}) fusion(f32[1771,2,2,128]{3,2,1,0:T(2,128)} %reshape.26), kind=kLoop, calls=%fused_computation.2 | loop fusion | bytes 7254016 | tf_op jit(solution)/shard_map/squeeze | solution.py:236
  9.7 3.7 %collective-permute-start.2 = (f32[1771,2,128]{2,1,0:T(2,128)}, f32[1771,2,128]{2,1,0:T(2,128)}, u32[]{:S(2)}, u32[]{:S(2)}) collective-permute-start(f32[1771,2,128]{2,1,0:T(2,128)} %get-tuple-element.5), channel_id=1, source_target_pairs={{0,1},{1,2},{2,3},{3,4},{4,5},{5,6},{6,7},{7,8},{8,9},{9,10},{10,1... | collective-permute-start | bytes 5440520 | tf_op jit(solution)/shard_map/ppermute | solution.py:236
  13.4 1.9 %collective-permute-start.3 = (f32[1771,2,128]{2,1,0:T(2,128)S(1)}, f32[1771,2,128]{2,1,0:T(2,128)}, u32[]{:S(2)}, u32[]{:S(2)}) collective-permute-start(f32[1771,2,128]{2,1,0:T(2,128)S(1)} %get-tuple-element.6), channel_id=1, source_target_pairs={{1,0},{2,1},{3,2},{4,3},{5,4},{6,5},{7,6},{8,7},{9,8},{10,9},{11,1... | collective-permute-start | bytes 5440520 | tf_op jit(solution)/shard_map/ppermute | solution.py:237
  15.3 0.0 copy-done
  15.3 0.1 reshape.28
  15.4 3.6 %collective-permute-start = (f32[21,2,128]{2,1,0:T(2,128)S(1)}, f32[21,2,128]{2,1,0:T(2,128)S(1)}, u32[]{:S(2)}, u32[]{:S(2)}) collective-permute-start(f32[21,2,128]{2,1,0:T(2,128)S(1)} %get-tuple-element.7), channel_id=1, source_target_pairs={{0,1},{1,2},{2,3},{3,4},{4,5},{5,6},{6,7},{7,8},{8,9},{9,10},{10,1... | collective-permute-start | bytes 64520 | tf_op jit(solution)/shard_map/ppermute | solution.py:236
  19.1 1.9 %collective-permute-start.1 = (f32[21,2,128]{2,1,0:T(2,128)S(1)}, f32[21,2,128]{2,1,0:T(2,128)S(1)}, u32[]{:S(2)}, u32[]{:S(2)}) collective-permute-start(f32[21,2,128]{2,1,0:T(2,128)S(1)} %get-tuple-element.8), channel_id=1, source_target_pairs={{1,0},{2,1},{3,2},{4,3},{5,4},{6,5},{7,6},{8,7},{9,8},{10,9},{11,1... | collective-permute-start | bytes 64520 | tf_op jit(solution)/shard_map/ppermute | solution.py:237
  21.0 32.4 %collective-permute-done = f32[21,2,128]{2,1,0:T(2,128)S(1)} collective-permute-done((f32[21,2,128]{2,1,0:T(2,128)S(1)}, f32[21,2,128]{2,1,0:T(2,128)S(1)}, u32[]{:S(2)}, u32[]{:S(2)}) %collective-permute-start) | collective-permute-done | bytes 21536 | tf_op jit(solution)/shard_map/ppermute | solution.py:236
  53.4 1.6 %collective-permute-done.1 = f32[21,2,128]{2,1,0:T(2,128)S(1)} collective-permute-done((f32[21,2,128]{2,1,0:T(2,128)S(1)}, f32[21,2,128]{2,1,0:T(2,128)S(1)}, u32[]{:S(2)}, u32[]{:S(2)}) %collective-permute-start.1) | collective-permute-done | bytes 21536 | tf_op jit(solution)/shard_map/ppermute | solution.py:237
  55.0 80.8 %local.1.refs_0_ = f32[1771,4,128]{2,1,0:T(4,128)S(1)} custom-call(f32[1771,4,128]{2,1,0:T(4,128)} %bitcast.41, f32[21,4,128]{2,1,0:T(4,128)S(1)} %bitcast.37, f32[21,4,128]{2,1,0:T(4,128)S(1)} %bitcast.39), custom_call_target="tpu_custom_call" | custom-call | flops 40000000 | bytes 40000000 | tf_op jit(solution)/shard_map/local/pallas_call | solution.py:255
  135.9 0.0 collective-permute-done.2
  135.9 0.0 collective-permute-done.3
  135.9 6.2 %pad_maximum_fusion = f32[1771,2,2,128]{3,2,1,0:T(2,128)} fusion(f32[1771,2,1,128]{3,2,1,0:T(1,128)} %bitcast.14, f32[1771,2,1,128]{3,2,1,0:T(1,128)} %bitcast.12), kind=kLoop, calls=%fused_computation | loop fusion | flops 906752 | bytes 7254016 | tf_op jit(solution)/shard_map/stack | solution.py:242
  142.1 8.8 %halo.1 = f32[1771,4,128]{2,1,0:T(4,128)} custom-call(f32[1771,4,128]{2,1,0:T(4,128)S(1)} %local.1.refs_0_, f32[1771,4,128]{2,1,0:T(4,128)} %bitcast.42, f32[21,4,128]{2,1,0:T(4,128)S(1)} %bitcast.38, f32[21,4,128]{2,1,0:T(4,128)S(1)} %bitcast.40), custom_call_target="tpu_custom_call" | custom-call | tf_op jit(solution)/shard_map/halo/pallas_call | solution.py:269
  (2 shorter events, 0.1 us)
Async XLA Ops:
  6.6 8.7 %copy-start = (f32[21,2,256]{2,1,0:T(2,128)S(1)}, f32[21,2,256]{2,1,0:T(2,128)}, u32[]{:S(2)}) copy-start(f32[21,2,256]{2,1,0:T(2,128)} %param.3) | copy-start | bytes 129028
  9.7 126.2 %collective-permute-start.2 = (f32[1771,2,128]{2,1,0:T(2,128)}, f32[1771,2,128]{2,1,0:T(2,128)}, u32[]{:S(2)}, u32[]{:S(2)}) collective-permute-start(f32[1771,2,128]{2,1,0:T(2,128)} %get-tuple-element.5), channel_id=1, source_target_pairs={{0,1},{1,2},{2,3},{3,4},{4,5},{5,6},{6,7},{7,8},{8,9},{9,10},{10,1... | collective-permute-start | bytes 5440520 | tf_op jit(solution)/shard_map/ppermute | solution.py:236
  13.4 122.5 %collective-permute-start.3 = (f32[1771,2,128]{2,1,0:T(2,128)S(1)}, f32[1771,2,128]{2,1,0:T(2,128)}, u32[]{:S(2)}, u32[]{:S(2)}) collective-permute-start(f32[1771,2,128]{2,1,0:T(2,128)S(1)} %get-tuple-element.6), channel_id=1, source_target_pairs={{1,0},{2,1},{3,2},{4,3},{5,4},{6,5},{7,6},{8,7},{9,8},{10,9},{11,1... | collective-permute-start | bytes 5440520 | tf_op jit(solution)/shard_map/ppermute | solution.py:237
  15.4 38.0 %collective-permute-start = (f32[21,2,128]{2,1,0:T(2,128)S(1)}, f32[21,2,128]{2,1,0:T(2,128)S(1)}, u32[]{:S(2)}, u32[]{:S(2)}) collective-permute-start(f32[21,2,128]{2,1,0:T(2,128)S(1)} %get-tuple-element.7), channel_id=1, source_target_pairs={{0,1},{1,2},{2,3},{3,4},{4,5},{5,6},{6,7},{7,8},{8,9},{9,10},{10,1... | collective-permute-start | bytes 64520 | tf_op jit(solution)/shard_map/ppermute | solution.py:236
  19.1 35.9 %collective-permute-start.1 = (f32[21,2,128]{2,1,0:T(2,128)S(1)}, f32[21,2,128]{2,1,0:T(2,128)S(1)}, u32[]{:S(2)}, u32[]{:S(2)}) collective-permute-start(f32[21,2,128]{2,1,0:T(2,128)S(1)} %get-tuple-element.8), channel_id=1, source_target_pairs={{1,0},{2,1},{3,2},{4,3},{5,4},{6,5},{7,6},{8,7},{9,8},{10,9},{11,1... | collective-permute-start | bytes 64520 | tf_op jit(solution)/shard_map/ppermute | solution.py:237

commit v2 on v1

--- a/solution.py
+++ b/solution.py
@@ -154,38 +154,134 @@
     )
 
 
-def local_kernel(modes, f_ref, c_ref, h_ref, o_ref, u_ref, w_ref, u2, acc_a, acc_b):
-    terms = 1 + VARS
+TERMS = 1 + VARS
+SLOTS = 24
+COEF = 4 * SLOTS
+BUILD = 8
+FIRST_VARS = (0, 2, 5, 9, VARS)
+
+
+def rounded(n, to):
+    return -(-n // to) * to
+
+
+def blocks(lo, hi, width, step):
+    groups = (hi - lo) // width
+    if groups > 0:
+        lax.fori_loop(0, groups, lambda n, c: (step(lo + n * width, width), c)[1], 0)
+    for n in range(lo + groups * width, hi):
+        step(n, 1)
+
+
+def fused_kernel(
+    modes, devices, f_ref, c_ref, o_ref,
+    rows, top, bottom, above, below, send_sem, recv_sem, u_ref, w_ref, d_ref, wh_ref,
+    u2, acc_a, acc_b, h2, hacc_a, hacc_b,
+):
+    me = lax.axis_index("grid")
+    has_up = me > 0
+    has_down = me < devices - 1
+    mesh_id = pl.DeviceIdType.MESH
+    barrier = pltpu.get_barrier_semaphore()
+
+    @pl.when(has_up)
+    def _():
+        pl.semaphore_signal(barrier, inc=1, device_id={"grid": me - 1}, device_id_type=mesh_id)
+
+    @pl.when(has_down)
+    def _():
+        pl.semaphore_signal(barrier, inc=1, device_id={"grid": me + 1}, device_id_type=mesh_id)
+
+    total_rows = rows.shape[0]
+    cuts = [0]
+    for i in FIRST_VARS[1:-1]:
+        cuts.append(rounded(2 * SLOTS + 2 * idx3(i, i, i), 8))
+    cuts.append(total_rows // 2)
+
+    def copies(n):
+        part = pl.ds(cuts[n], cuts[n + 1] - cuts[n])
+        going_up = pltpu.make_async_remote_copy(
+            src_ref=top.at[part], dst_ref=below.at[part],
+            send_sem=send_sem.at[0, n], recv_sem=recv_sem.at[0, n],
+            device_id={"grid": me - 1}, device_id_type=mesh_id,
+        )
+        going_down = pltpu.make_async_remote_copy(
+            src_ref=bottom.at[part], dst_ref=above.at[part],
+            send_sem=send_sem.at[1, n], recv_sem=recv_sem.at[1, n],
+            device_id={"grid": me + 1}, device_id_type=mesh_id,
+        )
+        return going_up, going_down
+
+    rows[0 : 4 * TERMS] = c_ref[...].reshape(4 * TERMS, LANES)
+    rows[4 * TERMS : COEF] = jnp.zeros((COEF - 4 * TERMS, LANES), jnp.float32)
+
+    def fill(n, count):
+        value = f_ref[pl.ds(4 * n, 4 * count)].reshape(16 * count, LANES)
+        rows[pl.ds(pl.multiple_of(COEF + 16 * n, 16), 16 * count)] = value
+
+    def pack(n, count):
+        for q in range(count):
+            at = 16 * (n + q)
+            low = rows[pl.ds(at, 8, stride=2)]
+            high = rows[pl.ds(at + 1, 8, stride=2)]
+            to = pl.ds(pl.multiple_of(8 * (n + q), 8), 8)
+            top[to] = low
+            bottom[to] = high
+
+    whole = modes // 4
+    done = 0
+    for n in range(len(cuts) - 1):
+        until = (cuts[n + 1] - 2 * SLOTS) // 8
+        blocks(done, min(until, whole), 4, fill)
+        if until > whole:
+            left = modes - 4 * whole
+            at = COEF + 16 * whole
+            rows[at : at + 4 * left] = f_ref[4 * whole : modes].reshape(4 * left, LANES)
+            rows[at + 4 * left : total_rows] = jnp.zeros(
+                (total_rows - at - 4 * left, LANES), jnp.float32
+            )
+        done = until
+        blocks(cuts[n] // 8, cuts[n + 1] // 8, 8, pack)
+        going_up, going_down = copies(n)
+        if n == 0:
+            pl.semaphore_wait(barrier, has_up.astype(jnp.int32) + has_down.astype(jnp.int32))
+
+        @pl.when(has_up)
+        def _():
+            going_up.start()
+
+        @pl.when(has_down)
+        def _():
+            going_down.start()
 
     def weights(n, _):
-        at = jnp.minimum(2 * n, terms - 2)
-        c = c_ref[pl.ds(at, 2)].reshape(8, LANES)
-        h = h_ref[pl.ds(at, 2)].reshape(8, LANES)
+        c = rows[pl.ds(pl.multiple_of(8 * n, 8), 8)]
         east, west, other = shifted(c)
-        center = 0.5 * (4.0 * c + east + west + other + h)
-        a0, a1 = spread(center, -0.5 * (c + east))
+        a0, a1 = spread(0.5 * (3.0 * c + east + west + other), -0.5 * (c + east))
         b0, b1 = spread(-0.5 * (c + west), -0.5 * (c + other))
-        w_ref[0, at] = a0
-        w_ref[0, at + 1] = a1
-        w_ref[1, at] = b0
-        w_ref[1, at + 1] = b1
+        w_ref[0, 2 * n] = a0
+        w_ref[0, 2 * n + 1] = a1
+        w_ref[1, 2 * n] = b0
+        w_ref[1, 2 * n + 1] = b1
         return 0
 
-    lax.fori_loop(0, (terms + 1) // 2, weights, 0)
-
-    def build(n, _):
-        at = jnp.minimum(2 * n, modes - 2)
-        g = f_ref[pl.ds(at, 2)].reshape(8, LANES)
-        east, west, other = shifted(g)
-        a0, a1 = spread(g, east)
-        b0, b1 = spread(west, other)
-        u_ref[0, at] = a0
-        u_ref[0, at + 1] = a1
-        u_ref[1, at] = b0
-        u_ref[1, at + 1] = b1
-        return 0
-
-    lax.fori_loop(0, (modes + 1) // 2, build, 0)
+    lax.fori_loop(0, (TERMS + 1) // 2, weights, 0)
+
+    def build(n, count):
+        made = []
+        for q in range(count):
+            g = rows[pl.ds(pl.multiple_of(COEF + 8 * (n + q), 8), 8)]
+            east, west, other = shifted(g)
+            made.append(spread(g, east) + spread(west, other))
+        for q in range(count):
+            a0, a1, b0, b1 = made[q]
+            at = 2 * (n + q)
+            u_ref[0, at] = a0
+            u_ref[0, at + 1] = a1
+            u_ref[1, at] = b0
+            u_ref[1, at + 1] = b1
+
+    blocks(0, (modes + 1) // 2, BUILD, build)
 
     def half(n, _):
         load = lambda m: u_ref[n, m]
@@ -201,25 +297,78 @@
 
     lax.fori_loop(0, 2, half, 0)
 
-    def total(m, _):
-        both = u_ref[0, m] + u_ref[1, m]
-        o_ref[m] = both[0:4] + both[4:8]
-        return 0
-
-    lax.fori_loop(0, modes, total, 0, unroll=7)
-
-
-def halo_kernel(modes, a_ref, g_ref, c_ref, h_ref, o_ref, w_ref, u2, acc_a, acc_b):
-    w_ref[...] = -0.5 * (c_ref[...] + h_ref[...])
-    load = lambda m: g_ref[m]
-    w = lambda t: w_ref[t]
+    def total(n, count):
+        made = []
+        for q in range(count):
+            both = u_ref[0, n + q] + u_ref[1, n + q]
+            made.append(both[0:4] + both[4:8])
+        for q in range(count):
+            o_ref[n + q] = made[q]
+
+    blocks(0, modes, 8, total)
+
+    @pl.when(jnp.logical_not(has_up))
+    def _():
+        above[...] = jnp.zeros_like(above)
+
+    @pl.when(jnp.logical_not(has_down))
+    def _():
+        below[...] = jnp.zeros_like(below)
+
+    def differ(n, count):
+        made = []
+        for q in range(count):
+            at = 16 * (n + q)
+            of = pl.ds(pl.multiple_of(8 * (n + q), 8), 8)
+            made.append(
+                (rows[pl.ds(at, 8, stride=2)] - above[of], rows[pl.ds(at + 1, 8, stride=2)] - below[of])
+            )
+        for q in range(count):
+            at = 16 * (n + q)
+            rows[pl.ds(at, 8, stride=2)] = made[q][0]
+            rows[pl.ds(at + 1, 8, stride=2)] = made[q][1]
+
+    def unfold(n, count):
+        value = rows[pl.ds(pl.multiple_of(COEF + 16 * n, 16), 16 * count)]
+        d_ref[pl.ds(4 * n, 4 * count)] = value.reshape(4 * count, 4, LANES)
+
+    load = lambda m: d_ref[m]
+    w = lambda t: wh_ref[t]
 
     def store(m, value):
-        o_ref[m] = a_ref[m] + value
-
-    out0 = start_low(load, w, u2, acc_a, acc_b, store)
-    cubic(load, w, u2, acc_a, acc_b, store, 0, VARS)
-    finish_low(out0, u2, acc_a, acc_b, store)
+        o_ref[m] = o_ref[m] + value
+
+    out0 = None
+    for n in range(len(cuts) - 1):
+        going_up, going_down = copies(n)
+
+        @pl.when(has_down)
+        def _():
+            going_up.wait_recv()
+
+        @pl.when(has_up)
+        def _():
+            going_down.wait_recv()
+
+        blocks(cuts[n] // 8, cuts[n + 1] // 8, 8, differ)
+        blocks(max(cuts[n] - 2 * SLOTS, 0) // 8, (cuts[n + 1] - 2 * SLOTS) // 8, 4, unfold)
+        if n == 0:
+            change = rows[0 : 4 * TERMS].reshape(TERMS, 4, LANES)
+            wh_ref[...] = c_ref[...] - 0.5 * change
+            out0 = start_low(load, w, h2, hacc_a, hacc_b, store)
+        cubic(load, w, h2, hacc_a, hacc_b, store, FIRST_VARS[n], FIRST_VARS[n + 1])
+    finish_low(out0, h2, hacc_a, hacc_b, store)
+
+    for n in range(len(cuts) - 1):
+        going_up, going_down = copies(n)
+
+        @pl.when(has_up)
+        def _():
+            going_up.wait_send()
+
+        @pl.when(has_down)
+        def _():
+            going_down.wait_send()
 
 
 def tiled(array):
@@ -227,57 +376,39 @@
     return array.reshape(n, 2, 2, LANES).transpose(0, 2, 1, 3).reshape(n, 4, LANES)
 
 
-def exchange(array):
-    size = lax.axis_size("grid")
-    up = [(i, i + 1) for i in range(size - 1)]
-    down = [(i + 1, i) for i in range(size - 1)]
-    n = array.shape[0]
-    four = array.reshape(n, 2, 2, LANES)
-    above = lax.ppermute(four[:, 1], "grid", up)
-    below = lax.ppermute(four[:, 0], "grid", down)
-    return above, below
-
-
-def merge(above, below):
-    return jnp.stack([above, below], axis=2).reshape(above.shape[0], 4, LANES)
-
-
-def body(field, coef):
+def body(devices, field, coef):
     modes = field.shape[0]
-    c4 = tiled(coef)
-    f4 = tiled(field)
-    hc = merge(*exchange(coef))
-    above, below = exchange(field)
-    params = pltpu.CompilerParams(vmem_limit_bytes=48 * 1024 * 1024)
-    low = lambda s: [pltpu.VMEM((NPAIR + VARS, s, LANES), jnp.float32)] + [
-        pltpu.VMEM((NPAIR, s, LANES), jnp.float32)
-    ] * 2
-    part = pl.pallas_call(
-        lambda *refs: local_kernel(modes, *refs),
+    even = rounded(modes, 4)
+    total_rows = COEF + 4 * even
+    chunks = len(FIRST_VARS) - 1
+    buf = lambda *shape: pltpu.VMEM(shape + (LANES,), jnp.float32)
+    low = lambda s: [buf(NPAIR + VARS, s), buf(NPAIR, s), buf(NPAIR, s)]
+    out = pl.pallas_call(
+        lambda *refs: fused_kernel(modes, devices, *refs),
         out_shape=jax.ShapeDtypeStruct((modes, 4, LANES), jnp.float32),
-        scratch_shapes=[
-            pltpu.VMEM((2, modes, 8, LANES), jnp.float32),
-            pltpu.VMEM((2, 1 + VARS, 8, LANES), jnp.float32),
-        ]
-        + low(8),
-        compiler_params=params,
-        cost_estimate=pl.CostEstimate(
-            flops=40 * 10**6, bytes_accessed=40 * 10**6, transcendentals=0
+        in_specs=[pl.BlockSpec(memory_space=pltpu.VMEM)] * 2,
+        out_specs=pl.BlockSpec(memory_space=pltpu.VMEM),
+        scratch_shapes=[buf(total_rows)]
+        + [buf(total_rows // 2)] * 4
+        + [pltpu.SemaphoreType.DMA((2, chunks))] * 2
+        + [buf(2, even, 8), buf(2, TERMS + 1, 8), buf(even, 4), buf(TERMS, 4)]
+        + low(8)
+        + low(4),
+        compiler_params=pltpu.CompilerParams(
+            collective_id=0, has_side_effects=True, vmem_limit_bytes=56 * 1024 * 1024
         ),
-        name="local",
-    )(f4, c4, hc)
-    out = pl.pallas_call(
-        lambda *refs: halo_kernel(modes, *refs),
-        out_shape=jax.ShapeDtypeStruct((modes, 4, LANES), jnp.float32),
-        scratch_shapes=[pltpu.VMEM((1 + VARS, 4, LANES), jnp.float32)] + low(4),
-        compiler_params=params,
-        name="halo",
-    )(part, merge(above, below), c4, hc)
+        name="fused",
+    )(tiled(field), tiled(coef))
     return out.reshape(modes, 2, 2, LANES).transpose(0, 2, 1, 3).reshape(field.shape)
 
 
 def solution(mesh):
     placed = P(None, ("parts", "grid"), None)
+    devices = mesh.shape["grid"]
     return jax.shard_map(
-        body, mesh=mesh, in_specs=(placed, placed), out_specs=placed, check_vma=False
+        lambda field, coef: body(devices, field, coef),
+        mesh=mesh,
+        in_specs=(placed, placed),
+        out_specs=placed,
+        check_vma=False,
     )

time: 151 us -> 53.7 us (0.36)
  Pallas kernels: 89.6 us -> 48.2 us
  waiting for transfers between devices: 34 us -> 0 us
  starting transfers between devices: 11.2 us -> 0 us
  other arithmetic: 6.22 us -> 0 us
  local copies, waits for them, and re-layouts: 9.76 us -> 5.31 us
    pallas_call x2 -> x1, Pallas kernels: 89.6 us -> 48.2 us  [body(): pl.pallas_call(lambda *refs: fused_kernel(modes, devices, *refs), out_sha...]
    ppermute x4 -> x0, waiting for transfers between devices: 34 us -> none  [the longest x2 32.4 us: exchange(): above = lax.ppermute(four[:, 1], 'grid', up)]
    ppermute x4 -> x0, starting transfers between devices: 11.2 us -> none  [the longest x2 7.34 us: exchange(): above = lax.ppermute(four[:, 1], 'grid', up)]
    reshape x2 -> x0, local copies, waits for them, and re-layouts: 6.68 us -> none  [tiled(): array.reshape(n, 2, 2, LANES).transpose(0, 2, 1, 3).reshape(n, 4, LANES)]
    another operation x2 -> x0, other arithmetic: 6.22 us -> none  [merge(): return jnp.stack([above, below], axis=2).reshape(above.shape[0], 4, LANES)]
    unnamed x2 -> x1, local copies, waits for them, and re-layouts: 0.01 us -> 5.31 us
    squeeze x2 -> x0, local copies, waits for them, and re-layouts: 3.08 us -> none  [exchange(): above = lax.ppermute(four[:, 1], 'grid', up)]
  transfers between devices with their start and end apart: 4 -> 0, of which waited for: 2 -> 0; matrix products, arithmetic and copies ran while one was open for 0% -> 0% of each run, Pallas kernels for 54% -> 0%
where the time goes in v2:
time: 53.7 us; the launch traced here: 53.5 us
  Pallas kernels  48.2 us (90%)
  local copies, waits for them, and re-layouts  5.31 us (10%)
    pallas_call x1, Pallas kernels, body(): pl.pallas_call(lambda *refs: fused_kernel(modes, devices, *refs), out_sha...  48.2 us
    unnamed x1, local copies, waits for them, and re-layouts  5.31 us

profile of v2, /device:TPU:9, one launch (start us, length us, event | category | flops | bytes accessed | tf_op | source)
XLA Modules:
  0.0 53.5 jit_solution(14745794250012400797)
XLA Ops:
  0.0 48.2 %fused.1 = f32[1771,4,128]{2,1,0:T(4,128)} custom-call(f32[1771,4,128]{2,1,0:T(4,128)} %bitcast.16, f32[21,4,128]{2,1,0:T(4,128)} %bitcast.17), custom_call_target="tpu_custom_call" | custom-call | tf_op jit(solution)/shard_map/fused/pallas_call | solution.py:386
  48.2 5.3 %copy.7 = f32[1771,2,256]{2,1,0:T(2,128)} copy(f32[1771,2,256]{2,1,0:T(2,128)} %bitcast.15) | data formatting | bytes 7254016

commit v3 on v2

--- a/solution.py
+++ b/solution.py
@@ -158,7 +158,7 @@
 SLOTS = 24
 COEF = 4 * SLOTS
 BUILD = 8
-FIRST_VARS = (0, 2, 5, 9, VARS)
+FIRST_VARS = (0, 1, 3, 6, 11, VARS)
 
 
 def rounded(n, to):
@@ -395,7 +395,7 @@
         + low(8)
         + low(4),
         compiler_params=pltpu.CompilerParams(
-            collective_id=0, has_side_effects=True, vmem_limit_bytes=56 * 1024 * 1024
+            collective_id=0, has_side_effects=True, vmem_limit_bytes=46 * 1024 * 1024
         ),
         name="fused",
     )(tiled(field), tiled(coef))

time: 53.7 us -> 48.7 us (0.907)
  Pallas kernels: 48.2 us -> 43.9 us
  local copies, waits for them, and re-layouts: 5.31 us -> 4.63 us
    pallas_call x1, Pallas kernels: 48.2 us -> 43.9 us  [body(): pl.pallas_call(lambda *refs: fused_kernel(modes, devices, *refs), out_sha...]
    unnamed x1 -> x5, local copies, waits for them, and re-layouts: 5.31 us -> 4.63 us
where the time goes in v3:
time: 48.7 us; the launch traced here: 48.5 us
  Pallas kernels  43.9 us (90%)
  local copies, waits for them, and re-layouts  4.63 us (10%)
    pallas_call x1, Pallas kernels, body(): pl.pallas_call(lambda *refs: fused_kernel(modes, devices, *refs), out_sha...  43.9 us
    unnamed x5, local copies, waits for them, and re-layouts  4.63 us

profile of v3, /device:TPU:9, one launch (start us, length us, event | category | flops | bytes accessed | tf_op | source)
XLA Modules:
  0.0 48.5 jit_solution(10140818677982435144)
XLA Ops:
  0.0 0.0 copy-start
  0.0 2.0 %copy-done = f32[1771,2,256]{2,1,0:T(2,128)S(1)} copy-done((f32[1771,2,256]{2,1,0:T(2,128)S(1)}, f32[1771,2,256]{2,1,0:T(2,128)}, u32[]{:S(2)}) %copy-start) | copy-done | bytes 3627032
  2.0 0.0 copy-start.1
  2.0 0.8 %copy-done.1 = f32[21,2,256]{2,1,0:T(2,128)S(1)} copy-done((f32[21,2,256]{2,1,0:T(2,128)S(1)}, f32[21,2,256]{2,1,0:T(2,128)}, u32[]{:S(2)}) %copy-start.1) | copy-done | bytes 43032
  2.8 43.9 %fused.1 = f32[1771,4,128]{2,1,0:T(4,128)S(1)} custom-call(f32[1771,4,128]{2,1,0:T(4,128)S(1)} %bitcast.16, f32[21,4,128]{2,1,0:T(4,128)S(1)} %bitcast.17), custom_call_target="tpu_custom_call" | custom-call | tf_op jit(solution)/shard_map/fused/pallas_call | solution.py:386
  46.7 1.8 %copy.7 = f32[1771,2,256]{2,1,0:T(2,128)} copy(f32[1771,2,256]{2,1,0:T(2,128)S(1)} %bitcast.15) | data formatting | bytes 7254016
Async XLA Ops:
  0.0 2.0 %copy-start = (f32[1771,2,256]{2,1,0:T(2,128)S(1)}, f32[1771,2,256]{2,1,0:T(2,128)}, u32[]{:S(2)}) copy-start(f32[1771,2,256]{2,1,0:T(2,128)} %param.2) | copy-start | bytes 10881028
  2.0 0.8 %copy-start.1 = (f32[21,2,256]{2,1,0:T(2,128)S(1)}, f32[21,2,256]{2,1,0:T(2,128)}, u32[]{:S(2)}) copy-start(f32[21,2,256]{2,1,0:T(2,128)} %param.3) | copy-start | bytes 129028
